TPU v7x, 128 devices: a whole 4x4x4 slice. The times are simulated.
128 devices in a mesh: group: 2 (over y_lo), resp: 8 (over y_hi, z), tensor: 8 (over x, core).
Axes of the slice: x: 4, y: 4 (y_hi: 2, y_lo: 2; y = y_hi * 2 + y_lo), z: 4, core: 2. Of those that a mesh axis runs over, the one named last changes fastest.
Arguments:
- queries: bfloat16 [16, 512, 8192], P(('group', 'resp'), None, 'tensor'), parts along dimension 0, may hold values from -50 to 50
- resp_keys: bfloat16 [16, 512, 1024], P(('group', 'resp'), None, 'tensor'), parts along dimension 0, may hold values from -6 to 6
- resp_values: bfloat16 [16, 512, 1024], P(('group', 'resp'), None, 'tensor'), parts along dimension 0, may hold values from -6 to 6
- prompt_keys: bfloat16 [4096, 1024], P(('group', 'resp', 'tensor')), parts along dimension 0, may hold values from -7 to 7
- prompt_values: bfloat16 [4096, 1024], P(('group', 'resp', 'tensor')), parts along dimension 0, may hold values from -6 to 6
- out_grad: bfloat16 [16, 512, 8192], P(('group', 'resp'), None, 'tensor'), parts along dimension 0, may hold values from -6 to 6
- lengths: int32 [16], P(('group', 'resp')), parts along dimension 0, may hold values from 1 to 512, 2560 in all
Outputs:
- attended: bfloat16 [16, 512, 8192], P(('group', 'resp'), None, 'tensor'), parts along dimension 0
- query_grad: bfloat16 [16, 512, 8192], P(('group', 'resp'), None, 'tensor'), parts along dimension 0
- resp_key_grad: bfloat16 [16, 512, 1024], P(('group', 'resp'), None, 'tensor'), parts along dimension 0
- resp_value_grad: bfloat16 [16, 512, 1024], P(('group', 'resp'), None, 'tensor'), parts along dimension 0
- prompt_key_grad: float32 [4096, 1024], P(('group', 'resp', 'tensor')), parts along dimension 0
- prompt_value_grad: float32 [4096, 1024], P(('group', 'resp', 'tensor')), parts along dimension 0
There are 2 independent parts, one for each index of `group`. A program takes and returns all parts, laid end to end along the dimension named above; each array names one. Nothing has to cross between parts.
Inputs may be any that keep to these rules, and one draw needn't show every extreme that they name: For each prompt group separately, its 8 lengths sum to 2560, and one of them is exactly 512; the table lists the groups one after another.
All inputs are finite; a program needn't handle non-finite values.
Results may differ from a plain program's by a relative error of at most 0.012.
The roundings to bfloat16 on the way count: a program that leaves them out, or rounds other values in their place, can miss the bound.
Values may be sent and summed in bfloat16 or wider, within the bound.
A program may use at most 64 MiB of HBM per device.

v0:
```python
import jax
import jax.numpy as jnp
from jax import lax
from jax.sharding import PartitionSpec as P

HD = 128


def head_slice(array, index, column, width):
    picked = lax.dynamic_index_in_dim(array, index, 0, keepdims=False)
    return lax.dynamic_slice_in_dim(picked, column, width, 1)


def add_block(running, term):
    return running + term


def per_device(queries, resp_keys, resp_values, prompt_keys, prompt_values, out_grad, lengths):
    member_count, seq_len, query_width = queries.shape
    pair_width = resp_keys.shape[2]
    query_heads = query_width // HD
    heads_per = query_heads // (pair_width // HD)
    block_count = member_count * query_heads
    factor = HD ** (-0.5)
    every_keys, every_values = (
        lax.all_gather(prompt_keys, ("resp", "tensor"), axis=0, tiled=True),
        lax.all_gather(prompt_values, ("resp", "tensor"), axis=0, tiled=True),
    )
    offset = lax.axis_index("tensor") * pair_width
    cache_keys = lax.dynamic_slice_in_dim(every_keys, offset, pair_width, 1)
    cache_values = lax.dynamic_slice_in_dim(every_values, offset, pair_width, 1)
    prompt_rows = cache_keys.shape[0]
    positions = jnp.arange(seq_len, dtype=jnp.int32)
    causal = positions[None, :] <= positions[:, None]

    def block_inputs(block_index):
        member = block_index // query_heads
        head_index = block_index % query_heads
        column = head_index // heads_per * HD
        query_rows = head_slice(queries, member, head_index * HD, HD)
        grad_rows = head_slice(out_grad, member, head_index * HD, HD)
        resp_length = lax.dynamic_index_in_dim(lengths, member, 0, keepdims=False)
        live_rows = (positions < resp_length)[:, None]
        live_grad = jnp.where(live_rows, grad_rows, jnp.zeros_like(grad_rows))
        return (member, head_index, column, query_rows, live_grad, live_rows, resp_length)

    def main_step(block_index, state_tuple):
        (
            attended,
            query_grad,
            key_running,
            value_running,
            prompt_key_running,
            prompt_value_running,
            row_tops,
            row_totals,
            row_deltas,
        ) = state_tuple
        member, head_index, column, query_rows, live_grad, live_rows, resp_length = block_inputs(
            block_index
        )
        key_resp = head_slice(resp_keys, member, column, HD)
        value_resp = head_slice(resp_values, member, column, HD)
        allowed = causal & (positions[None, :] < resp_length)
        score_prompt = (
            jnp.einsum("qd,kd->qk", query_rows, cache_keys, preferred_element_type=jnp.float32)
            * factor
        )
        score_resp = jnp.where(
            allowed,
            jnp.einsum("qd,kd->qk", query_rows, key_resp, preferred_element_type=jnp.float32)
            * factor,
            -jnp.inf,
        )
        row_top = jnp.maximum(jnp.max(score_prompt, 1), jnp.max(score_resp, 1))
        exp_prompt = jnp.exp(score_prompt - row_top[:, None])
        exp_resp = jnp.exp(score_resp - row_top[:, None])
        row_total = jnp.sum(exp_prompt, 1) + jnp.sum(exp_resp, 1)
        frac_prompt = exp_prompt / row_total[:, None]
        frac_resp = exp_resp / row_total[:, None]
        weight_prompt = frac_prompt.astype(jnp.bfloat16)
        weight_resp = frac_resp.astype(jnp.bfloat16)
        mixture = jnp.dot(
            weight_prompt, cache_values, preferred_element_type=jnp.float32
        ) + jnp.dot(weight_resp, value_resp, preferred_element_type=jnp.float32)
        out_block = jnp.where(live_rows, mixture, 0.0).astype(jnp.bfloat16)
        row_delta = jnp.sum(
            live_grad.astype(jnp.float32) * lax.optimization_barrier(out_block).astype(jnp.float32),
            1,
        )
        dprob_prompt = jnp.einsum(
            "qd,kd->qk", live_grad, cache_values, preferred_element_type=jnp.float32
        )
        dprob_resp = jnp.einsum(
            "qd,kd->qk", live_grad, value_resp, preferred_element_type=jnp.float32
        )
        sgrad_prompt = (frac_prompt * (dprob_prompt - row_delta[:, None])).astype(jnp.bfloat16)
        sgrad_resp = (frac_resp * (dprob_resp - row_delta[:, None])).astype(jnp.bfloat16)
        block_qgrad = (
            factor
            * (
                jnp.dot(sgrad_prompt, cache_keys, preferred_element_type=jnp.float32)
                + jnp.dot(sgrad_resp, key_resp, preferred_element_type=jnp.float32)
            )
        ).astype(jnp.bfloat16)
        key_term = factor * jnp.einsum(
            "qk,qd->kd", sgrad_resp, query_rows, preferred_element_type=jnp.float32
        )
        value_term = jnp.einsum(
            "qk,qd->kd", weight_resp, live_grad, preferred_element_type=jnp.float32
        )
        attended = lax.dynamic_update_slice(attended, out_block[None], (member, 0, head_index * HD))
        query_grad = lax.dynamic_update_slice(
            query_grad, block_qgrad[None], (member, 0, head_index * HD)
        )
        key_running = add_block(key_running, key_term[None])
        value_running = add_block(value_running, value_term[None])
        prompt_key_term = factor * jnp.einsum(
            "qk,qd->kd", sgrad_prompt, query_rows, preferred_element_type=jnp.float32
        )
        prompt_value_term = jnp.einsum(
            "qk,qd->kd", weight_prompt, live_grad, preferred_element_type=jnp.float32
        )
        prompt_key_running = add_block(prompt_key_running, prompt_key_term)
        prompt_value_running = add_block(prompt_value_running, prompt_value_term)
        return (
            attended,
            query_grad,
            key_running,
            value_running,
            prompt_key_running,
            prompt_value_running,
            row_tops,
            row_totals,
            row_deltas,
        )

    prompt_start = jnp.zeros((prompt_rows, pair_width), jnp.float32)
    stats_start = jnp.zeros((0,), jnp.float32)
    start_state = (
        jnp.zeros_like(queries),
        jnp.zeros_like(queries),
        jnp.zeros(resp_keys.shape, jnp.float32),
        jnp.zeros(resp_keys.shape, jnp.float32),
        prompt_start,
        prompt_start,
        stats_start,
        stats_start,
        stats_start,
    )
    final_state = lax.fori_loop(0, block_count, main_step, start_state)
    (
        attended,
        query_grad,
        key_running,
        value_running,
        prompt_key_running,
        prompt_value_running,
        row_tops,
        row_totals,
        row_deltas,
    ) = final_state
    key_sum, value_sum = (
        lax.psum_scatter(prompt_key_running, "resp", scatter_dimension=0, tiled=True),
        lax.psum_scatter(prompt_value_running, "resp", scatter_dimension=0, tiled=True),
    )
    key_grad, value_grad = (
        lax.all_to_all(key_sum, "tensor", split_axis=0, concat_axis=1, tiled=True),
        lax.all_to_all(value_sum, "tensor", split_axis=0, concat_axis=1, tiled=True),
    )
    return (
        attended,
        query_grad,
        key_running.astype(jnp.bfloat16),
        value_running.astype(jnp.bfloat16),
        key_grad,
        value_grad,
    )


def solution(mesh):
    placed = (
        P(("group", "resp"), None, "tensor"),
        P(("group", "resp"), None, "tensor"),
        P(("group", "resp"), None, "tensor"),
        P(("group", "resp", "tensor"), None),
        P(("group", "resp", "tensor"), None),
        P(("group", "resp"), None, "tensor"),
        P(("group", "resp")),
    )
    return jax.shard_map(
        per_device,
        mesh=mesh,
        in_specs=placed,
        out_specs=(
            P(("group", "resp"), None, "tensor"),
            P(("group", "resp"), None, "tensor"),
            P(("group", "resp"), None, "tensor"),
            P(("group", "resp"), None, "tensor"),
            P(("group", "resp", "tensor"), None),
            P(("group", "resp", "tensor"), None),
        ),
        check_vma=False,
    )
```

profile of v0, /device:TPU:1, one launch (start us, length us, event | category | flops | bytes accessed | tf_op | source)
XLA Modules:
  0.0 452.1 jit_solution(14350130730649730733)
XLA Ops:
  8.8 78.1 %all-gather.3.cloned.1.call-done = bf16[2048,1024]{1,0:T(8,128)(2,1)} async-done(((bf16[32,1024]{1,0:T(8,128)(2,1)}), bf16[2048,1024]{1,0:T(8,128)(2,1)}) %all-gather.3.cloned.1.call-update) | async-done | bytes 4194320 | tf_op jit(solution)/shard_map/all_gather | solution.py:26
  86.9 1.1 constant_dynamic-slice_fusion.1
  88.0 71.0 %all-gather.5.cloned.1.call-done = bf16[2048,1024]{1,0:T(8,128)(2,1)} async-done(((bf16[32,1024]{1,0:T(8,128)(2,1)}), bf16[2048,1024]{1,0:T(8,128)(2,1)}) %all-gather.5.cloned.1.call-update) | async-done | bytes 4194320 | tf_op jit(solution)/shard_map/all_gather | solution.py:27
  158.9 1.1 constant_dynamic-slice_fusion
  160.0 1.1 broadcast.95.clone
  161.1 1.1 broadcast.95
  162.2 128.4 %while.26 = (s32[]{:T(128)}, bf16[1,512,1024]{2,1,0:T(8,128)(2,1)}, bf16[1,512,1024]{2,1,0:T(8,128)(2,1)}, f32[1,512,128]{2,1,0:T(8,128)}, f32[1,512,128]{2,1,0:...) while((s32[]{:T(128)}, bf16[1,512,1024]{2,1,0:T(8,128)(2,1)}, ...), condition=%wide.region_6.7_spmd.clone, body=%wide.region_0.6_spmd.clone.sunk | while | flops 2033449984 | bytes 60471756 | solution.py:151
  162.8 1.2 fusion.110
  164.1 1.7 multiply_reduce_fusion.4
  169.3 1.0 bitcast_dynamic-update-slice_fusion.2
  171.0 1.3 fusion.119
  172.3 1.4 convolution_add_fusion.4
  175.2 2.1 fusion.121
  178.9 1.2 fusion.110
  180.1 1.7 multiply_reduce_fusion.4
  187.1 1.3 fusion.119
  188.4 1.4 convolution_add_fusion.4
  191.2 2.1 fusion.121
  195.0 1.2 fusion.110
  196.2 1.7 multiply_reduce_fusion.4
  203.1 1.3 fusion.119
  204.4 1.4 convolution_add_fusion.4
  207.3 2.1 fusion.121
  209.4 1.0 fusion.118
  211.0 1.2 fusion.110
  212.3 1.7 multiply_reduce_fusion.4
  217.5 1.0 bitcast_dynamic-update-slice_fusion.2
  219.2 1.3 fusion.119
  220.5 1.4 convolution_add_fusion.4
  223.4 2.1 fusion.121
  227.1 1.2 fusion.110
  228.3 1.7 multiply_reduce_fusion.4
  235.2 1.3 fusion.119
  236.5 1.4 convolution_add_fusion.4
  239.4 2.1 fusion.121
  241.5 1.0 fusion.118
  243.1 1.2 fusion.110
  244.4 1.7 multiply_reduce_fusion.4
  249.6 1.0 bitcast_dynamic-update-slice_fusion.2
  251.3 1.2 fusion.119
  252.6 1.4 convolution_add_fusion.4
  255.4 2.1 fusion.121
  257.5 1.0 fusion.118
  259.2 1.2 fusion.110
  260.4 1.7 multiply_reduce_fusion.4
  265.6 1.0 bitcast_dynamic-update-slice_fusion.2
  267.4 1.3 fusion.119
  268.6 1.4 convolution_add_fusion.4
  271.5 2.1 fusion.121
  273.6 1.0 fusion.118
  275.2 1.2 fusion.110
  276.5 1.7 multiply_reduce_fusion.4
  281.7 1.0 bitcast_dynamic-update-slice_fusion.2
  283.4 1.3 fusion.119
  284.7 1.4 convolution_add_fusion.4
  287.5 2.1 fusion.121
  289.6 1.0 fusion.118
  290.6 1.0 copy-done
  292.3 65.9 %reduce-scatter.3.cloned.1.call-done = f32[256,128]{1,0:T(8,128)} async-done(((f32[2048,128]{1,0:T(8,128)}), f32[256,128]{1,0:T(8,128)}) %reduce-scatter.3.cloned.1.call-update) | async-done | bytes 131088 | tf_op jit(solution)/shard_map/reduce_scatter | solution.py:164
  358.2 6.8 %all-to-all-start = ((f32[8,32,128]{2,1,0:T(8,128)}), f32[8,32,128]{2,1,0:T(8,128)S(1)}, u32[]{:S(2)}, u32[]{:S(2)}) async-start(f32[8,32,128]{2,1,0:T(8,128)} %bitcast.133), calls=%async_computation.1 | async-start | bytes 262144 | tf_op jit(solution)/shard_map/all_to_all | solution.py:168
  365.0 1.6 convert_element_type.86
  367.3 65.6 %reduce-scatter.5.cloned.1.call-done = f32[256,128]{1,0:T(8,128)} async-done(((f32[2048,128]{1,0:T(8,128)}), f32[256,128]{1,0:T(8,128)}) %reduce-scatter.5.cloned.1.call-update) | async-done | bytes 131088 | tf_op jit(solution)/shard_map/reduce_scatter | solution.py:165
  432.9 6.7 %all-to-all-start.1 = ((f32[8,32,128]{2,1,0:T(8,128)}), f32[8,32,128]{2,1,0:T(8,128)S(1)}, u32[]{:S(2)}, u32[]{:S(2)}) async-start(f32[8,32,128]{2,1,0:T(8,128)} %bitcast.132), calls=%async_computation.3 | async-start | bytes 262144 | tf_op jit(solution)/shard_map/all_to_all | solution.py:169
  440.3 4.6 %all-to-all-done.1 = f32[8,32,128]{2,1,0:T(8,128)S(1)} async-done(((f32[8,32,128]{2,1,0:T(8,128)}), f32[8,32,128]{2,1,0:T(8,128)S(1)}, u32[]{:S(2)}, u32[]{:S(2)}) %all-to-all-start.1) | async-done | bytes 131104 | tf_op jit(solution)/shard_map/all_to_all | solution.py:169
  (195 shorter events, 60.3 us)
Async XLA Ops:
  7.2 155.0 %copy-start.5 = (bf16[1,512,128]{2,1,0:T(8,128)(2,1)S(1)}, bf16[1,512,128]{2,1,0:T(8,128)(2,1)}, u32[]{:S(2)}) copy-start(bf16[1,512,128]{2,1,0:T(8,128)(2,1)} %param.10) | copy-start | bytes 393220
  7.2 79.7 %all-gather.3.cloned.1.call-start = ((), (), s32[]{:S(2)}) async-start(), calls=%async_computation.4 | async-start | bytes 4259840 | tf_op jit(solution)/shard_map/all_gather | solution.py:26
  7.9 151.0 %all-gather.5.cloned.1.call-start = ((), (), s32[]{:S(2)}) async-start(), calls=%async_computation.5 | async-start | bytes 4259840 | tf_op jit(solution)/shard_map/all_gather | solution.py:27
  8.7 349.5 %reduce-scatter.3.cloned.1.call-start = ((), (), s32[]{:S(2)}) async-start(), calls=%async_computation.6 | async-start | bytes 1179648 | tf_op jit(solution)/shard_map/reduce_scatter | solution.py:164
  167.7 1.2 copy-start.4
  167.7 1.6 copy-start.6
  168.4 2.6 copy-start.2
  172.3 2.2 copy-start.3
  183.7 1.2 copy-start.4
  183.7 1.6 copy-start.6
  184.5 2.6 copy-start.2
  188.3 2.2 copy-start.3
  199.8 1.2 copy-start.4
  199.8 1.6 copy-start.6
  200.5 2.6 copy-start.2
  204.4 2.2 copy-start.3
  215.8 1.2 copy-start.4
  215.9 1.6 copy-start.6
  216.6 2.6 copy-start.2
  220.5 2.2 copy-start.3
  231.9 1.2 copy-start.4
  231.9 1.6 copy-start.6
  232.6 2.6 copy-start.2
  236.5 2.1 copy-start.3
  247.9 1.2 copy-start.4
  248.0 1.6 copy-start.6
  248.7 2.6 copy-start.2
  252.6 2.2 copy-start.3
  264.0 1.2 copy-start.4
  264.0 1.6 copy-start.6
  264.7 2.6 copy-start.2
  268.6 2.2 copy-start.3
  280.0 1.2 copy-start.4
  280.1 1.6 copy-start.6
  280.8 2.6 copy-start.2
  284.7 2.1 copy-start.3
  290.6 1.0 copy-start
  290.6 1.3 copy-start.1
  291.7 141.2 %reduce-scatter.5.cloned.1.call-start = ((), (), s32[]{:S(2)}) async-start(), calls=%async_computation.7 | async-start | bytes 1179648 | tf_op jit(solution)/shard_map/reduce_scatter | solution.py:165
  358.2 74.7 %all-to-all-start = ((f32[8,32,128]{2,1,0:T(8,128)}), f32[8,32,128]{2,1,0:T(8,128)S(1)}, u32[]{:S(2)}, u32[]{:S(2)}) async-start(f32[8,32,128]{2,1,0:T(8,128)} %bitcast.133), calls=%async_computation.1 | async-start | bytes 262144 | tf_op jit(solution)/shard_map/all_to_all | solution.py:168
  432.9 12.0 %all-to-all-start.1 = ((f32[8,32,128]{2,1,0:T(8,128)}), f32[8,32,128]{2,1,0:T(8,128)S(1)}, u32[]{:S(2)}, u32[]{:S(2)}) async-start(f32[8,32,128]{2,1,0:T(8,128)} %bitcast.132), calls=%async_computation.3 | async-start | bytes 262144 | tf_op jit(solution)/shard_map/all_to_all | solution.py:169
Sparse Core Ops, SparseCore 0:
  11.2 75.6 all-gather.2
  90.0 68.8 all-gather.4
  291.8 66.3 reduce-scatter.2
  362.1 70.8 reduce-scatter.4
where the time goes:
time: 453 us; the launch traced here: 452 us
  waiting for transfers between devices  287 us (63%)
  matrix products  101 us (22%)
  other arithmetic  25.6 us (6%)
  between operations  13.8 us (3%)
  starting transfers between devices  13.7 us (3%)
  local copies, waits for them, and re-layouts  9.54 us (2%)
    all_gather x1, waiting for transfers between devices, per_device(): lax.all_gather(prompt_keys, ('resp', 'tensor'), axis=0, tiled=True)  78.1 us
    all_gather x1, waiting for transfers between devices, per_device(): lax.all_gather(prompt_values, ('resp', 'tensor'), axis=0, tiled=True)  71 us
    reduce_scatter x1, waiting for transfers between devices, per_device(): lax.psum_scatter(prompt_key_running, 'resp', scatter_dimension=0, tiled=T...  65.9 us
    reduce_scatter x1, waiting for transfers between devices, per_device(): lax.psum_scatter(prompt_value_running, 'resp', scatter_dimension=0, tiled...  65.6 us
    dot_general x8, matrix products, main_step(): jnp.einsum('qk,qd->kd', sgrad_prompt, query_rows, preferred_element_type=...  16.5 us
    dot_general x8, matrix products, main_step(): jnp.einsum('qd,kd->qk', query_rows, cache_keys, preferred_element_type=jn...  13.6 us
    dot_general x8, matrix products, main_step(): jnp.einsum('qk,qd->kd', weight_prompt, live_grad, preferred_element_type=...  10.9 us
    dot_general x8, matrix products, main_step(): jnp.einsum('qk,qd->kd', sgrad_resp, query_rows, preferred_element_type=jn...  10 us
  transfers between devices with their start and end apart: 6, of which 5 were waited for; matrix products, arithmetic and copies ran while one was open for 1% of the time, Pallas kernels for 0%

commit v1 on v0

v1 whole, which is shorter than its diff:
```python
import functools
import math

import jax
import jax.numpy as jnp
from jax import lax
from jax.experimental import pallas as pl
from jax.experimental.pallas import tpu as pltpu
from jax.sharding import PartitionSpec as P

HD = 128
CHUNK = 256
PAIR = 2
ONES = 16
SCALE = HD**-0.5
LOG_SCALE = SCALE / math.log(2.0)
BF16 = jnp.bfloat16
F32 = jnp.float32
MESH = pl.DeviceIdType.MESH


def mm(left, right):
    return jnp.dot(left, right, preferred_element_type=F32)


def by_tile(op, wide, stat):
    rows, lanes = wide.shape
    return op(wide.reshape(rows // 8, 8, lanes), stat[None]).reshape(rows, lanes)


def top_of(wide):
    rows, lanes = wide.shape
    return jnp.max(wide.reshape(rows // 8, 8, lanes), axis=0)


def hop(step, z_size):
    inner = step % z_size
    return step // z_size, ((inner + 1) // 2) * (2 * (inner % 2) - 1)


def kernel(
    sizes,
    length_ref,
    q_hbm,
    g_hbm,
    rk_hbm,
    rv_hbm,
    pk_hbm,
    pv_hbm,
    att_hbm,
    dq_hbm,
    drk_ref,
    drv_ref,
    dpk_ref,
    dpv_ref,
    q,
    g,
    rk,
    rv,
    q_t,
    g_t,
    k_t,
    v_t,
    k_two,
    cache,
    weights,
    tops,
    top,
    inv_total,
    delta,
    out_t,
    dq_t,
    att,
    dq,
    score_buf,
    w_buf,
    ds_buf,
    stat_a,
    stat_b,
    acc,
    send_buf,
    recv_buf,
    total,
    in_sem,
    out_sem,
    a_send,
    a_recv,
    b_send,
    b_recv,
    c_send,
    c_recv,
    d_send,
    d_recv,
):
    n_resp, n_tensor, z_size, heads = sizes
    y_size = n_resp // z_size
    seq = q.shape[0]
    share = pk_hbm.shape[0]
    resp = lax.axis_index("resp")
    tensor = lax.axis_index("tensor")
    y, z = resp // z_size, resp % z_size

    def sends_to(step):
        dy, dz = hop(step, z_size)
        return ((y + dy) % y_size) * z_size + (z + dz + z_size) % z_size

    def comes_from(step):
        dy, dz = hop(step, z_size)
        return ((y - dy + y_size) % y_size) * z_size + (z - dz + z_size) % z_size

    def columns(index):
        return pl.ds(pl.multiple_of(index * HD, HD), HD)

    def part(index):
        return pl.ds(pl.multiple_of(index * share, share), share)

    loads = [
        pltpu.make_async_copy(source, target, in_sem.at[index])
        for index, (source, target) in enumerate(
            (
                (q_hbm, q),
                (g_hbm, g),
                (rk_hbm, rk),
                (rv_hbm, rv),
                (pk_hbm.at[:, columns(tensor)], cache.at[resp, 0, part(tensor)]),
                (pv_hbm.at[:, columns(tensor)], cache.at[resp, 1, part(tensor)]),
            )
        )
    ]
    for load in loads:
        load.start()

    barrier = pltpu.get_barrier_semaphore()

    def greet_tensor(step, carry):
        pl.semaphore_signal(
            barrier, inc=1, device_id={"tensor": (tensor + step) % n_tensor}, device_id_type=MESH
        )
        return carry

    def greet_resp(step, carry):
        pl.semaphore_signal(
            barrier, inc=1, device_id={"resp": sends_to(step)}, device_id_type=MESH
        )
        return carry

    lax.fori_loop(1, n_tensor, greet_tensor, 0)
    lax.fori_loop(1, n_resp, greet_resp, 0)
    pl.semaphore_wait(barrier, n_tensor - 1 + n_resp - 1)

    def spread(step, which):
        peer = (tensor + step) % n_tensor
        source = (pk_hbm, pv_hbm)[which]
        return pltpu.make_async_remote_copy(
            src_ref=source.at[:, columns(peer)],
            dst_ref=cache.at[resp, which, part(tensor)],
            send_sem=a_send.at[step, which],
            recv_sem=a_recv.at[step, which],
            device_id={"tensor": peer},
            device_id_type=MESH,
        )

    def gather(step):
        return pltpu.make_async_remote_copy(
            src_ref=cache.at[resp],
            dst_ref=cache.at[resp],
            send_sem=b_send.at[step],
            recv_sem=b_recv.at[step],
            device_id={"resp": sends_to(step)},
            device_id_type=MESH,
        )

    def start_spread(step, carry):
        spread(step, 0).start()
        spread(step, 1).start()
        return carry

    lax.fori_loop(1, n_tensor, start_spread, 0)

    length = length_ref[0]
    live_rows = lax.broadcasted_iota(jnp.int32, (seq, 1), 0) < length
    live_lanes = lax.broadcasted_iota(jnp.int32, (1, seq), 1) < length

    for load in loads:
        load.wait()

    def prepare_head(head, carry):
        wide = q[:, columns(head)].astype(F32).T * LOG_SCALE
        high = wide.astype(BF16)
        q_t[head, 0:HD] = high
        q_t[head, HD:] = (wide - high.astype(F32)).astype(BF16)
        live = jnp.where(live_rows, g[:, columns(head)], jnp.zeros((), BF16))
        g[:, columns(head)] = live
        g_t[head] = live.T
        return carry

    lax.fori_loop(0, heads, prepare_head, 0)

    def wait_spread(step, carry):
        spread(step, 0).wait()
        spread(step, 1).wait()
        return carry

    lax.fori_loop(1, n_tensor, wait_spread, 0)

    def start_gather(step, carry):
        gather(step).start()
        return carry

    lax.fori_loop(1, n_resp, start_gather, 0)

    def prepare_keys(step, keys, values):
        k_t[step] = keys.T
        v_t[step, 0:HD] = values.T
        v_t[step, HD:] = jnp.ones((ONES, CHUNK), BF16)
        rows = pl.ds(pl.multiple_of(step * CHUNK, CHUNK), CHUNK)
        k_two[rows, 0:HD] = keys
        k_two[rows, HD:] = keys

    key_at = lax.broadcasted_iota(jnp.int32, (CHUNK, CHUNK), 0)
    row_at = lax.broadcasted_iota(jnp.int32, (CHUNK, CHUNK), 1)
    seen = key_at <= row_at

    blocks = seq // CHUNK
    for block in range(blocks):
        rows = slice(block * CHUNK, (block + 1) * CHUNK)
        prepare_keys(n_resp + block, rk[rows, :], rv[rows, :])

    def staged(stages):
        depth = len(stages)
        for turn in range(heads + depth - 1):
            for late, stage in enumerate(stages):
                if 0 <= turn - late < heads:
                    stage(turn - late)

    def own_scores(head):
        slot = head % 2
        tops_of = [None] * blocks
        for block in range(blocks):
            for lane in range(block, blocks):
                lanes = slice(lane * CHUNK, (lane + 1) * CHUNK)
                rows = slice(block * CHUNK, (block + 1) * CHUNK)
                at = (n_resp + block) * CHUNK
                score = mm(k_two[at : at + CHUNK, :], q_t[head, :, lanes])
                if lane == block:
                    score = jnp.where(seen, score, -jnp.inf)
                score_buf[slot, rows, lanes] = score
                block_top = top_of(score)
                old = tops_of[lane]
                tops_of[lane] = block_top if old is None else jnp.maximum(old, block_top)
        highest = jnp.concatenate(tops_of, axis=1)
        highest = jnp.broadcast_to(jnp.max(highest, axis=0, keepdims=True), highest.shape)
        top[head] = highest
        for block in range(blocks):
            tops[n_resp + block, head] = highest

    def own_weights(head):
        slot = head % 2
        for block in range(blocks):
            lanes = slice(block * CHUNK, seq)
            rows = slice(block * CHUNK, (block + 1) * CHUNK)
            shift = tops[n_resp + block, head, :, lanes]
            power = jnp.exp2(by_tile(jnp.subtract, score_buf[slot, rows, lanes], shift))
            weights[n_resp + block, head, :, lanes] = power.astype(BF16)

    def own_mix(head):
        for block in range(blocks):
            lanes = slice(block * CHUNK, seq)
            term = mm(v_t[n_resp + block], weights[n_resp + block, head, :, lanes])
            if block == 0:
                out_t[head] = term
            else:
                out_t[head, :, lanes] += term

    staged((own_scores, own_weights, own_mix))

    def forward(turn, carry):
        first = turn * PAIR
        for index in range(PAIR):
            step = first + index

            @pl.when(step > 0)
            def _():
                gather(step).wait_recv()

            source = comes_from(step)
            prepare_keys(step, cache[source, 0], cache[source, 1])

        def scores(head):
            slot = head % 2
            highest = None
            for index in range(PAIR):
                at = pl.ds(pl.multiple_of((first + index) * CHUNK, CHUNK), CHUNK)
                score = mm(k_two[at, :], q_t[head])
                score_buf[slot, index * CHUNK : (index + 1) * CHUNK] = score
                block_top = top_of(score)
                highest = block_top if highest is None else jnp.maximum(highest, block_top)
            old = top[head]
            new = jnp.maximum(old, jnp.max(highest, axis=0, keepdims=True))
            top[head] = new
            stat_a[slot] = jnp.exp2(old - new)
            for index in range(PAIR):
                tops[first + index, head] = new

        def powers(head):
            slot = head % 2
            shift = tops[first, head]
            for index in range(PAIR):
                score = score_buf[slot, index * CHUNK : (index + 1) * CHUNK]
                power = jnp.exp2(by_tile(jnp.subtract, score, shift))
                weights[first + index, head] = power.astype(BF16)
            stat_b[slot] = stat_a[slot]

        def mix(head):
            term = mm(v_t[first], weights[first, head])
            for index in range(1, PAIR):
                term = term + mm(v_t[first + index], weights[first + index, head])
            out_t[head] = by_tile(jnp.multiply, out_t[head], stat_b[head % 2]) + term

        staged((scores, powers, mix))
        return carry

    lax.fori_loop(0, n_resp // PAIR, forward, 0)

    def close_head(head, carry):
        inverse = 1.0 / out_t[head, HD : HD + 1]
        inv_total[head] = jnp.broadcast_to(inverse, (8, seq))
        done = jnp.where(live_lanes, out_t[head, 0:HD] * inverse, 0.0).astype(BF16)
        row_delta = jnp.sum(
            done.astype(F32) * g_t[head].astype(F32), axis=0, keepdims=True
        )
        delta[head] = jnp.broadcast_to(row_delta, (8, seq))
        att[:, columns(head)] = done.T
        dq_t[head] = jnp.zeros((HD, seq), F32)
        return carry

    lax.fori_loop(0, heads, close_head, 0)
    att_out = pltpu.make_async_copy(att, att_hbm, out_sem.at[0])
    att_out.start()

    def backward_chunk(step, values, low):
        lanes = slice(low, seq)
        width = seq - low

        def products(head):
            slot = head % 2
            score_buf[slot, 0:CHUNK, 0:width] = mm(values, g_t[head, :, lanes])
            stat_a[slot, :, 0:width] = (
                jnp.exp2(tops[step, head, :, lanes] - top[head, :, lanes])
                * inv_total[head, :, lanes]
            )

        def grads(head):
            slot = head % 2
            weight = by_tile(
                jnp.multiply,
                weights[step, head, :, lanes].astype(F32),
                stat_a[slot, :, 0:width],
            )
            w_buf[slot, :, 0:width] = weight.astype(BF16)
            gap = by_tile(
                jnp.subtract, score_buf[slot, 0:CHUNK, 0:width], delta[head, :, lanes]
            )
            ds_buf[slot, :, 0:width] = (weight * gap).astype(BF16)

        def terms(head):
            slot = head % 2
            score_grad = ds_buf[slot, :, 0:width]
            dq_t[head, :, lanes] += mm(k_t[step], score_grad)
            at = slice(head * HD, (head + 1) * HD)
            key_term = mm(score_grad, q[lanes, at])
            value_term = mm(w_buf[slot, :, 0:width], g[lanes, at])
            if head == 0:
                acc[0] = key_term
                acc[1] = value_term
            else:
                acc[0] += key_term
                acc[1] += value_term

        staged((products, grads, terms))

    def collect(step):
        return pltpu.make_async_remote_copy(
            src_ref=send_buf.at[step],
            dst_ref=recv_buf.at[step],
            send_sem=c_send.at[step],
            recv_sem=c_recv.at[step],
            device_id={"resp": comes_from(step)},
            device_id_type=MESH,
        )

    def backward(turn, carry):
        step = n_resp - 1 - turn
        backward_chunk(step, cache[comes_from(step), 1], 0)

        @pl.when(step > 0)
        def _():
            send_buf[step, 0] = (acc[0] * SCALE).astype(BF16)
            send_buf[step, 1] = acc[1].astype(BF16)
            collect(step).start()

        @pl.when(step == 0)
        def _():
            total[0] = acc[0] * SCALE
            total[1] = acc[1]

        return carry

    lax.fori_loop(0, n_resp, backward, 0)

    for block in range(blocks):
        rows = slice(block * CHUNK, (block + 1) * CHUNK)
        backward_chunk(n_resp + block, rv[rows, :], block * CHUNK)
        drk_ref[rows, :] = (acc[0] * SCALE).astype(BF16)
        drv_ref[rows, :] = acc[1].astype(BF16)

    def add_part(step, carry):
        collect(step).wait()
        total[0] += recv_buf[step, 0].astype(F32)
        total[1] += recv_buf[step, 1].astype(F32)
        return carry

    lax.fori_loop(1, n_resp, add_part, 0)

    def give_back(step, which):
        peer = (tensor + step) % n_tensor
        target = (dpk_ref, dpv_ref)[which]
        return pltpu.make_async_remote_copy(
            src_ref=total.at[which, part(peer)],
            dst_ref=target.at[:, columns(tensor)],
            send_sem=d_send.at[step, which],
            recv_sem=d_recv.at[step, which],
            device_id={"tensor": peer},
            device_id_type=MESH,
        )

    def start_give(step, carry):
        give_back(step, 0).start()
        give_back(step, 1).start()
        return carry

    lax.fori_loop(1, n_tensor, start_give, 0)
    dpk_ref[:, columns(tensor)] = total[0, part(tensor), :]
    dpv_ref[:, columns(tensor)] = total[1, part(tensor), :]

    def close_query(head, carry):
        dq[:, columns(head)] = (dq_t[head] * SCALE).astype(BF16).T
        return carry

    lax.fori_loop(0, heads, close_query, 0)
    dq_out = pltpu.make_async_copy(dq, dq_hbm, out_sem.at[1])
    dq_out.start()

    def wait_give(step, carry):
        give_back(step, 0).wait()
        give_back(step, 1).wait()
        return carry

    lax.fori_loop(1, n_tensor, wait_give, 0)

    def wait_gather(step, carry):
        gather(step).wait_send()
        return carry

    lax.fori_loop(1, n_resp, wait_gather, 0)
    att_out.wait()
    dq_out.wait()


def per_device(
    n_resp, n_tensor, queries, resp_keys, resp_values, prompt_keys, prompt_values, out_grad, lengths
):
    _, seq, width = queries.shape
    heads = width // HD
    share, wide = prompt_keys.shape
    blocks = seq // CHUNK
    steps = n_resp + blocks
    hbm = pl.BlockSpec(memory_space=pl.ANY)
    vmem = pl.BlockSpec(memory_space=pltpu.VMEM)
    dma = pltpu.SemaphoreType.DMA
    shape = jax.ShapeDtypeStruct
    z_size = 4 if n_resp % 4 == 0 else n_resp
    results = pl.pallas_call(
        functools.partial(kernel, (n_resp, n_tensor, z_size, heads)),
        out_shape=(
            shape((seq, width), BF16),
            shape((seq, width), BF16),
            shape((seq, HD), BF16),
            shape((seq, HD), BF16),
            shape((share, wide), F32),
            shape((share, wide), F32),
        ),
        in_specs=[pl.BlockSpec(memory_space=pltpu.SMEM)] + [hbm] * 6,
        out_specs=(hbm, hbm, vmem, vmem, vmem, vmem),
        scratch_shapes=[
            pltpu.VMEM((seq, width), BF16),
            pltpu.VMEM((seq, width), BF16),
            pltpu.VMEM((seq, HD), BF16),
            pltpu.VMEM((seq, HD), BF16),
            pltpu.VMEM((heads, 2 * HD, seq), BF16),
            pltpu.VMEM((heads, HD, seq), BF16),
            pltpu.VMEM((steps, HD, CHUNK), BF16),
            pltpu.VMEM((steps, HD + ONES, CHUNK), BF16),
            pltpu.VMEM((steps * CHUNK, 2 * HD), BF16),
            pltpu.VMEM((n_resp, 2, CHUNK, HD), BF16),
            pltpu.VMEM((steps, heads, CHUNK, seq), BF16),
            pltpu.VMEM((steps, heads, 8, seq), F32),
            pltpu.VMEM((heads, 8, seq), F32),
            pltpu.VMEM((heads, 8, seq), F32),
            pltpu.VMEM((heads, 8, seq), F32),
            pltpu.VMEM((heads, HD + ONES, seq), F32),
            pltpu.VMEM((heads, HD, seq), F32),
            pltpu.VMEM((seq, width), BF16),
            pltpu.VMEM((seq, width), BF16),
            pltpu.VMEM((2, max(PAIR * CHUNK, seq), seq), F32),
            pltpu.VMEM((2, CHUNK, seq), BF16),
            pltpu.VMEM((2, CHUNK, seq), BF16),
            pltpu.VMEM((2, 8, seq), F32),
            pltpu.VMEM((2, 8, seq), F32),
            pltpu.VMEM((2, CHUNK, HD), F32),
            pltpu.VMEM((n_resp, 2, CHUNK, HD), BF16),
            pltpu.VMEM((n_resp, 2, CHUNK, HD), BF16),
            pltpu.VMEM((2, CHUNK, HD), F32),
            dma((6,)),
            dma((2,)),
            dma((n_tensor, 2)),
            dma((n_tensor, 2)),
            dma((n_resp,)),
            dma((n_resp,)),
            dma((n_resp,)),
            dma((n_resp,)),
            dma((n_tensor, 2)),
            dma((n_tensor, 2)),
        ],
        compiler_params=pltpu.CompilerParams(
            collective_id=0, has_side_effects=True, vmem_limit_bytes=60 * 2**20
        ),
    )(
        lengths,
        queries[0],
        out_grad[0],
        resp_keys[0],
        resp_values[0],
        prompt_keys,
        prompt_values,
    )
    attended, query_grad, key_grad, value_grad, prompt_key_grad, prompt_value_grad = results
    return (
        attended[None],
        query_grad[None],
        key_grad[None],
        value_grad[None],
        prompt_key_grad,
        prompt_value_grad,
    )


def solution(mesh):
    rows = P(("group", "resp"), None, "tensor")
    cached = P(("group", "resp", "tensor"), None)
    return jax.shard_map(
        functools.partial(per_device, mesh.shape["resp"], mesh.shape["tensor"]),
        mesh=mesh,
        in_specs=(rows, rows, rows, cached, cached, rows, P(("group", "resp"))),
        out_specs=(rows, rows, rows, rows, cached, cached),
        check_vma=False,
    )
```

time: 453 us -> 72.1 us (0.16)
  waiting for transfers between devices: 287 us -> 0 us
  matrix products: 101 us -> 0 us
  Pallas kernels: 0 us -> 63.5 us
  other arithmetic: 25.6 us -> 0 us
  starting transfers between devices: 13.7 us -> 0 us
  between operations: 13.8 us -> 1.3 us
    all_gather x2 -> x0, waiting for transfers between devices: 149 us -> none  [the longest x1 78.1 us: per_device(): lax.all_gather(prompt_keys, ('resp', 'tensor'), axis=0, tiled=True)]
    reduce_scatter x2 -> x0, waiting for transfers between devices: 132 us -> none  [the longest x1 65.9 us: per_device(): lax.psum_scatter(prompt_key_running, 'resp', scatter_dimension=0, tiled=T...]
    dot_general x96 -> x0, matrix products: 101 us -> none  [the longest x8 16.5 us: main_step(): jnp.einsum('qk,qd->kd', sgrad_prompt, query_rows, preferred_element_type=...]
    pallas_call x0 -> x1, Pallas kernels: none -> 63.5 us  [per_device(): pl.pallas_call(functools.partial(kernel, (n_resp, n_tensor, z_size, heads...]
    all_to_all x2 -> x0, starting transfers between devices: 13.5 us -> none  [the longest x1 6.81 us: per_device(): lax.all_to_all(key_sum, 'tensor', split_axis=0, concat_axis=1, tiled=True)]
    reduce_sum x24 -> x0, other arithmetic: 10 us -> none  [the longest x16 8.14 us: main_step(): row_total = jnp.sum(exp_prompt, 1) + jnp.sum(exp_resp, 1)]
    div x8 -> x0, other arithmetic: 6.67 us -> none  [main_step(): frac_prompt = exp_prompt / row_total[:, None]]
    unnamed x6 -> x16, local copies, waits for them, and re-layouts: 1.28 us -> 6.88 us
  transfers between devices with their start and end apart: 6 -> 0, of which waited for: 5 -> 0; matrix products, arithmetic and copies ran while one was open for 1% -> 0% of each run, Pallas kernels for 0% -> 0%
where the time goes in v1:
time: 72.1 us; the launch traced here: 71.7 us
  Pallas kernels  63.5 us (88%)
  local copies, waits for them, and re-layouts  6.88 us (10%)
  between operations  1.3 us (2%)
    pallas_call x1, Pallas kernels, per_device(): pl.pallas_call(functools.partial(kernel, (n_resp, n_tensor, z_size, heads...  63.5 us
    unnamed x16, local copies, waits for them, and re-layouts  6.88 us

profile of v1, /device:TPU:1, one launch (start us, length us, event | category | flops | bytes accessed | tf_op | source)
XLA Modules:
  0.0 71.7 jit_solution(5138059529619017895)
XLA Ops:
  1.3 63.5 %shard_map.118 = (bf16[512,1024]{1,0:T(8,128)(2,1)}, bf16[512,1024]{1,0:T(8,128)(2,1)}, bf16[512,128]{1,0:T(8,128)(2,1)}, bf16[512,128]{1,0:T(8,128)(2,1)}, f32[32,1024]{1,0:T(8,128)}, /*index=5*/f32[32,1024]{1,0:T(8,128)}) custom-call(s32[1]{0:T(128)S(6)} %copy.19.length_ref, bf16[512,1024]{1,0:T(8,128)(2,1)} %bitcast.8, bf16[512,1024]{1,0:T(8,128)(2,1)} %bitcast.9, ...), custom_call_target="tpu_custom_call" | custom-call | tf_op jit(solution)/shard_map/pallas_call | solution.py:483
  64.8 0.0 copy-start
  64.8 2.4 %copy.20 = bf16[1,512,1024]{2,1,0:T(8,128)(2,1)} copy(bf16[1,512,1024]{2,1,0:T(8,128)(2,1)} %bitcast.11) | data formatting | bytes 2097152
  67.1 0.0 copy-done
  67.1 0.0 copy-start.4
  67.1 1.0 %copy.21 = bf16[1,512,1024]{2,1,0:T(8,128)(2,1)} copy(bf16[1,512,1024]{2,1,0:T(8,128)(2,1)S(1)} %bitcast.10) | data formatting | bytes 2097152
  68.1 0.1 copy-done.4
  68.2 0.0 copy-start.3
  68.2 0.7 copy.22
  68.8 0.3 copy-done.3
  69.1 0.0 copy-start.2
  69.1 0.7 copy.23
  69.8 0.3 copy-done.2
  70.1 0.0 copy-start.1
  70.1 0.7 copy.24
  70.7 0.3 copy-done.1
  71.0 0.7 copy.25
Async XLA Ops:
  64.8 2.4 %copy-start = (bf16[512,1024]{1,0:T(8,128)(2,1)S(1)}, bf16[512,1024]{1,0:T(8,128)(2,1)}, u32[]{:S(2)}) copy-start(bf16[512,1024]{1,0:T(8,128)(2,1)} %get-tuple-element.13) | copy-start | bytes 3145732
  67.1 1.0 %copy-start.4 = (bf16[512,128]{1,0:T(8,128)(2,1)S(1)}, bf16[512,128]{1,0:T(8,128)(2,1)}, u32[]{:S(2)}) copy-start(bf16[512,128]{1,0:T(8,128)(2,1)} %get-tuple-element.14) | copy-start | bytes 393220
  68.2 1.0 %copy-start.3 = (bf16[512,128]{1,0:T(8,128)(2,1)S(1)}, bf16[512,128]{1,0:T(8,128)(2,1)}, u32[]{:S(2)}) copy-start(bf16[512,128]{1,0:T(8,128)(2,1)} %get-tuple-element.15) | copy-start | bytes 393220
  69.1 1.0 %copy-start.2 = (f32[32,1024]{1,0:T(8,128)S(1)}, f32[32,1024]{1,0:T(8,128)}, u32[]{:S(2)}) copy-start(f32[32,1024]{1,0:T(8,128)} %get-tuple-element.28) | copy-start | bytes 393220
  70.1 1.0 %copy-start.1 = (f32[32,1024]{1,0:T(8,128)S(1)}, f32[32,1024]{1,0:T(8,128)}, u32[]{:S(2)}) copy-start(f32[32,1024]{1,0:T(8,128)} %get-tuple-element.29) | copy-start | bytes 393220

commit v2 on v1

--- a/solution.py
+++ b/solution.py
@@ -12,6 +12,7 @@
 CHUNK = 256
 PAIR = 2
 ONES = 16
+VMEM_BYTES = 54 * 2**20
 SCALE = HD**-0.5
 LOG_SCALE = SCALE / math.log(2.0)
 BF16 = jnp.bfloat16
@@ -47,12 +48,11 @@
     rv_hbm,
     pk_hbm,
     pv_hbm,
-    att_hbm,
-    dq_hbm,
+    att,
+    dq,
     drk_ref,
     drv_ref,
-    dpk_ref,
-    dpv_ref,
+    dp_ref,
     q,
     g,
     rk,
@@ -70,8 +70,6 @@
     delta,
     out_t,
     dq_t,
-    att,
-    dq,
     score_buf,
     w_buf,
     ds_buf,
@@ -81,8 +79,10 @@
     send_buf,
     recv_buf,
     total,
+    own_kv,
+    rounded,
+    returned,
     in_sem,
-    out_sem,
     a_send,
     a_recv,
     b_send,
@@ -108,6 +108,9 @@
         dy, dz = hop(step, z_size)
         return ((y - dy + y_size) % y_size) * z_size + (z - dz + z_size) % z_size
 
+    def chunk_at(dy, dz):
+        return ((y + dy) % y_size) * z_size + (z + dz + z_size) % z_size
+
     def columns(index):
         return pl.ds(pl.multiple_of(index * HD, HD), HD)
 
@@ -118,12 +121,12 @@
         pltpu.make_async_copy(source, target, in_sem.at[index])
         for index, (source, target) in enumerate(
             (
+                (pk_hbm, own_kv.at[0]),
+                (pv_hbm, own_kv.at[1]),
                 (q_hbm, q),
                 (g_hbm, g),
                 (rk_hbm, rk),
                 (rv_hbm, rv),
-                (pk_hbm.at[:, columns(tensor)], cache.at[resp, 0, part(tensor)]),
-                (pv_hbm.at[:, columns(tensor)], cache.at[resp, 1, part(tensor)]),
             )
         )
     ]
@@ -132,47 +135,85 @@
 
     barrier = pltpu.get_barrier_semaphore()
 
+    def greet(target):
+        pl.semaphore_signal(barrier, inc=1, device_id=target, device_id_type=MESH)
+
     def greet_tensor(step, carry):
-        pl.semaphore_signal(
-            barrier, inc=1, device_id={"tensor": (tensor + step) % n_tensor}, device_id_type=MESH
-        )
+        peer = (tensor + step) % n_tensor
+        greet({"tensor": peer})
+        greet({"tensor": peer, "resp": chunk_at(0, 1)})
+        greet({"tensor": peer, "resp": chunk_at(0, -1)})
         return carry
 
     def greet_resp(step, carry):
-        pl.semaphore_signal(
-            barrier, inc=1, device_id={"resp": sends_to(step)}, device_id_type=MESH
-        )
+        greet({"resp": sends_to(step)})
         return carry
 
     lax.fori_loop(1, n_tensor, greet_tensor, 0)
     lax.fori_loop(1, n_resp, greet_resp, 0)
-    pl.semaphore_wait(barrier, n_tensor - 1 + n_resp - 1)
-
-    def spread(step, which):
+    loads[0].wait()
+    loads[1].wait()
+    pl.semaphore_wait(barrier, 3 * (n_tensor - 1) + n_resp - 1)
+
+    def spread(side, step):
         peer = (tensor + step) % n_tensor
-        source = (pk_hbm, pv_hbm)[which]
+        target = {"tensor": peer}
+        if side:
+            target["resp"] = chunk_at(0, (0, 1, -1)[side])
         return pltpu.make_async_remote_copy(
-            src_ref=source.at[:, columns(peer)],
-            dst_ref=cache.at[resp, which, part(tensor)],
-            send_sem=a_send.at[step, which],
-            recv_sem=a_recv.at[step, which],
+            src_ref=own_kv.at[:, :, columns(peer)],
+            dst_ref=cache.at[resp, :, part(tensor)],
+            send_sem=a_send.at[side, step],
+            recv_sem=a_recv.at[side, step],
+            device_id=target,
+            device_id_type=MESH,
+        )
+
+    def arrival(side, step):
+        peer = (tensor - step + n_tensor) % n_tensor
+        chunk = cache.at[chunk_at(0, (0, -1, 1)[side]), :, part(peer)]
+        return pltpu.make_async_remote_copy(
+            src_ref=chunk,
+            dst_ref=chunk,
+            send_sem=a_send.at[side, step],
+            recv_sem=a_recv.at[side, step],
             device_id={"tensor": peer},
             device_id_type=MESH,
         )
 
-    def gather(step):
+    def relay(slot, chunk, dy, dz):
         return pltpu.make_async_remote_copy(
-            src_ref=cache.at[resp],
-            dst_ref=cache.at[resp],
-            send_sem=b_send.at[step],
-            recv_sem=b_recv.at[step],
-            device_id={"resp": sends_to(step)},
+            src_ref=cache.at[chunk],
+            dst_ref=cache.at[chunk],
+            send_sem=b_send.at[slot],
+            recv_sem=b_recv.at[slot],
+            device_id={"resp": chunk_at(dy, dz)},
             device_id_type=MESH,
         )
 
+    routes = {
+        3: (chunk_at(0, 0), chunk_at(0, 2), 0, 2),
+        4: (chunk_at(0, 0), chunk_at(1, 0), 1, 0),
+        5: (chunk_at(1, 0), chunk_at(1, -1), 0, 1),
+        6: (chunk_at(1, 0), chunk_at(1, 1), 0, -1),
+        7: (chunk_at(0, 2), chunk_at(1, 2), 1, 0),
+    }
+    relays = {slot: relay(slot, out, dy, dz) for slot, (out, _, dy, dz) in routes.items()}
+    arrivals = {slot: relay(slot, got, dy, dz) for slot, (_, got, dy, dz) in routes.items()}
+
+    def pass_on(waited, begun):
+        for slot in waited:
+            arrivals[slot].wait_recv()
+        for slot in begun:
+            relays[slot].start()
+
     def start_spread(step, carry):
-        spread(step, 0).start()
-        spread(step, 1).start()
+        spread(0, step).start()
+        return carry
+
+    def start_sides(step, carry):
+        spread(1, step).start()
+        spread(2, step).start()
         return carry
 
     lax.fori_loop(1, n_tensor, start_spread, 0)
@@ -181,7 +222,9 @@
     live_rows = lax.broadcasted_iota(jnp.int32, (seq, 1), 0) < length
     live_lanes = lax.broadcasted_iota(jnp.int32, (1, seq), 1) < length
 
-    for load in loads:
+    cache[resp, 0, part(tensor), :] = own_kv[0, :, columns(tensor)]
+    cache[resp, 1, part(tensor), :] = own_kv[1, :, columns(tensor)]
+    for load in loads[2:]:
         load.wait()
 
     def prepare_head(head, carry):
@@ -195,19 +238,18 @@
         return carry
 
     lax.fori_loop(0, heads, prepare_head, 0)
+    lax.fori_loop(0, n_tensor, start_sides, 0)
 
     def wait_spread(step, carry):
-        spread(step, 0).wait()
-        spread(step, 1).wait()
-        return carry
-
-    lax.fori_loop(1, n_tensor, wait_spread, 0)
-
-    def start_gather(step, carry):
-        gather(step).start()
-        return carry
-
-    lax.fori_loop(1, n_resp, start_gather, 0)
+        spread(0, step).wait_send()
+        arrival(0, step).wait_recv()
+        return carry
+
+    def wait_sides(step, carry):
+        for side in (1, 2):
+            spread(side, step).wait_send()
+            arrival(side, step).wait_recv()
+        return carry
 
     def prepare_keys(step, keys, values):
         k_t[step] = keys.T
@@ -226,6 +268,12 @@
         rows = slice(block * CHUNK, (block + 1) * CHUNK)
         prepare_keys(n_resp + block, rk[rows, :], rv[rows, :])
 
+    lax.fori_loop(1, n_tensor, wait_spread, 0)
+    pass_on((), (3, 4))
+    prepare_keys(0, cache[resp, 0], cache[resp, 1])
+
+    near = [(0, 0, False)] + [(n_resp + block, block * CHUNK, True) for block in range(blocks)]
+
     def staged(stages):
         depth = len(stages)
         for turn in range(heads + depth - 1):
@@ -235,61 +283,53 @@
 
     def own_scores(head):
         slot = head % 2
-        tops_of = [None] * blocks
-        for block in range(blocks):
-            for lane in range(block, blocks):
+        highest = [None] * blocks
+        for index, (step, low, diagonal) in enumerate(near):
+            rows = slice(index * CHUNK, (index + 1) * CHUNK)
+            keys = k_two[step * CHUNK : (step + 1) * CHUNK, :]
+            for lane in range(low // CHUNK, blocks):
                 lanes = slice(lane * CHUNK, (lane + 1) * CHUNK)
-                rows = slice(block * CHUNK, (block + 1) * CHUNK)
-                at = (n_resp + block) * CHUNK
-                score = mm(k_two[at : at + CHUNK, :], q_t[head, :, lanes])
-                if lane == block:
+                score = mm(keys, q_t[head, :, lanes])
+                if diagonal and lane * CHUNK == low:
                     score = jnp.where(seen, score, -jnp.inf)
                 score_buf[slot, rows, lanes] = score
                 block_top = top_of(score)
-                old = tops_of[lane]
-                tops_of[lane] = block_top if old is None else jnp.maximum(old, block_top)
-        highest = jnp.concatenate(tops_of, axis=1)
+                old = highest[lane]
+                highest[lane] = block_top if old is None else jnp.maximum(old, block_top)
+        highest = jnp.concatenate(highest, axis=1)
         highest = jnp.broadcast_to(jnp.max(highest, axis=0, keepdims=True), highest.shape)
         top[head] = highest
-        for block in range(blocks):
-            tops[n_resp + block, head] = highest
+        for step, _, _ in near:
+            tops[step, head] = highest
 
     def own_weights(head):
         slot = head % 2
-        for block in range(blocks):
-            lanes = slice(block * CHUNK, seq)
-            rows = slice(block * CHUNK, (block + 1) * CHUNK)
-            shift = tops[n_resp + block, head, :, lanes]
-            power = jnp.exp2(by_tile(jnp.subtract, score_buf[slot, rows, lanes], shift))
-            weights[n_resp + block, head, :, lanes] = power.astype(BF16)
+        for index, (step, low, _) in enumerate(near):
+            rows = slice(index * CHUNK, (index + 1) * CHUNK)
+            shift = tops[step, head, :, low:seq]
+            power = jnp.exp2(by_tile(jnp.subtract, score_buf[slot, rows, low:seq], shift))
+            weights[step, head, :, low:seq] = power.astype(BF16)
 
     def own_mix(head):
-        for block in range(blocks):
-            lanes = slice(block * CHUNK, seq)
-            term = mm(v_t[n_resp + block], weights[n_resp + block, head, :, lanes])
-            if block == 0:
+        for index, (step, low, _) in enumerate(near):
+            term = mm(v_t[step], weights[step, head, :, low:seq])
+            if index == 0:
                 out_t[head] = term
             else:
-                out_t[head, :, lanes] += term
+                out_t[head, :, low:seq] += term
 
     staged((own_scores, own_weights, own_mix))
 
-    def forward(turn, carry):
-        first = turn * PAIR
-        for index in range(PAIR):
+    def forward(first, count):
+        for index in range(count):
             step = first + index
-
-            @pl.when(step > 0)
-            def _():
-                gather(step).wait_recv()
-
             source = comes_from(step)
             prepare_keys(step, cache[source, 0], cache[source, 1])
 
         def scores(head):
             slot = head % 2
             highest = None
-            for index in range(PAIR):
+            for index in range(count):
                 at = pl.ds(pl.multiple_of((first + index) * CHUNK, CHUNK), CHUNK)
                 score = mm(k_two[at, :], q_t[head])
                 score_buf[slot, index * CHUNK : (index + 1) * CHUNK] = score
@@ -299,13 +339,13 @@
             new = jnp.maximum(old, jnp.max(highest, axis=0, keepdims=True))
             top[head] = new
             stat_a[slot] = jnp.exp2(old - new)
-            for index in range(PAIR):
+            for index in range(count):
                 tops[first + index, head] = new
 
         def powers(head):
             slot = head % 2
             shift = tops[first, head]
-            for index in range(PAIR):
+            for index in range(count):
                 score = score_buf[slot, index * CHUNK : (index + 1) * CHUNK]
                 power = jnp.exp2(by_tile(jnp.subtract, score, shift))
                 weights[first + index, head] = power.astype(BF16)
@@ -313,14 +353,30 @@
 
         def mix(head):
             term = mm(v_t[first], weights[first, head])
-            for index in range(1, PAIR):
+            for index in range(1, count):
                 term = term + mm(v_t[first + index], weights[first + index, head])
             out_t[head] = by_tile(jnp.multiply, out_t[head], stat_b[head % 2]) + term
 
         staged((scores, powers, mix))
-        return carry
-
-    lax.fori_loop(0, n_resp // PAIR, forward, 0)
+
+    lax.fori_loop(0, n_tensor, wait_sides, 0)
+
+    def forward_single(step, carry):
+        pl.when(step == 2)(functools.partial(pass_on, (4,), (5, 6)))
+        forward(step, 1)
+        return carry
+
+    lax.fori_loop(1, 3, forward_single, 0)
+
+    def forward_turn(turn, carry):
+        pl.when(turn == 0)(functools.partial(pass_on, (3,), (7,)))
+        pl.when(turn == 1)(functools.partial(pass_on, (5, 6), ()))
+        forward(3 + turn * PAIR, PAIR)
+        return carry
+
+    lax.fori_loop(0, 2, forward_turn, 0)
+    pass_on((7,), ())
+    forward(n_resp - 1, 1)
 
     def close_head(head, carry):
         inverse = 1.0 / out_t[head, HD : HD + 1]
@@ -335,10 +391,7 @@
         return carry
 
     lax.fori_loop(0, heads, close_head, 0)
-    att_out = pltpu.make_async_copy(att, att_hbm, out_sem.at[0])
-    att_out.start()
-
-    def backward_chunk(step, values, low):
+    def backward_chunk(step, values, low, *more):
         lanes = slice(low, seq)
         width = seq - low
 
@@ -377,7 +430,7 @@
                 acc[0] += key_term
                 acc[1] += value_term
 
-        staged((products, grads, terms))
+        staged((products, grads, terms) + more)
 
     def collect(step):
         return pltpu.make_async_remote_copy(
@@ -408,11 +461,14 @@
 
     lax.fori_loop(0, n_resp, backward, 0)
 
-    for block in range(blocks):
+    def backward_own(block, *more):
         rows = slice(block * CHUNK, (block + 1) * CHUNK)
-        backward_chunk(n_resp + block, rv[rows, :], block * CHUNK)
+        backward_chunk(n_resp + block, rv[rows, :], block * CHUNK, *more)
         drk_ref[rows, :] = (acc[0] * SCALE).astype(BF16)
         drv_ref[rows, :] = acc[1].astype(BF16)
+
+    for block in range(1, blocks):
+        backward_own(block)
 
     def add_part(step, carry):
         collect(step).wait()
@@ -421,50 +477,55 @@
         return carry
 
     lax.fori_loop(1, n_resp, add_part, 0)
-
-    def give_back(step, which):
+    rounded[...] = total[...].astype(BF16)
+
+    def give_back(step):
         peer = (tensor + step) % n_tensor
-        target = (dpk_ref, dpv_ref)[which]
         return pltpu.make_async_remote_copy(
-            src_ref=total.at[which, part(peer)],
-            dst_ref=target.at[:, columns(tensor)],
-            send_sem=d_send.at[step, which],
-            recv_sem=d_recv.at[step, which],
+            src_ref=rounded.at[:, part(peer)],
+            dst_ref=returned.at[:, :, columns(tensor)],
+            send_sem=d_send.at[step],
+            recv_sem=d_recv.at[step],
             device_id={"tensor": peer},
             device_id_type=MESH,
         )
 
     def start_give(step, carry):
-        give_back(step, 0).start()
-        give_back(step, 1).start()
+        give_back(step).start()
         return carry
 
     lax.fori_loop(1, n_tensor, start_give, 0)
-    dpk_ref[:, columns(tensor)] = total[0, part(tensor), :]
-    dpv_ref[:, columns(tensor)] = total[1, part(tensor), :]
-
-    def close_query(head, carry):
-        dq[:, columns(head)] = (dq_t[head] * SCALE).astype(BF16).T
-        return carry
-
-    lax.fori_loop(0, heads, close_query, 0)
-    dq_out = pltpu.make_async_copy(dq, dq_hbm, out_sem.at[1])
-    dq_out.start()
+    returned[0, :, columns(tensor)] = rounded[0, part(tensor), :]
+    returned[1, :, columns(tensor)] = rounded[1, part(tensor), :]
+
+    def close_query(head):
+        dq[:, head * HD : (head + 1) * HD] = (dq_t[head] * SCALE).astype(BF16).T
+
+    backward_own(0, close_query)
 
     def wait_give(step, carry):
-        give_back(step, 0).wait()
-        give_back(step, 1).wait()
+        give_back(step).wait()
         return carry
 
     lax.fori_loop(1, n_tensor, wait_give, 0)
-
-    def wait_gather(step, carry):
-        gather(step).wait_send()
-        return carry
-
-    lax.fori_loop(1, n_resp, wait_gather, 0)
-    att_out.wait()
-    dq_out.wait()
+    dp_ref[...] = returned[...].astype(F32)
+
+    for copy in relays.values():
+        copy.wait_send()
+
+
+def deliver(att, dq, drk, drv, dp, *rest):
+    outputs, sems = rest[:-1], rest[-1]
+    copies = [
+        pltpu.make_async_copy(source, target, sems.at[index])
+        for index, (source, target) in enumerate(
+            zip((att, dq, drk, drv, dp.at[0], dp.at[1]), outputs)
+        )
+    ]
+    for copy in copies:
+        copy.start()
+    for copy in copies:
+        copy.wait()
 
 
 def per_device(
@@ -480,18 +541,20 @@
     dma = pltpu.SemaphoreType.DMA
     shape = jax.ShapeDtypeStruct
     z_size = 4 if n_resp % 4 == 0 else n_resp
+    outputs = (
+        ((seq, width), BF16),
+        ((seq, width), BF16),
+        ((seq, HD), BF16),
+        ((seq, HD), BF16),
+        ((share, wide), F32),
+        ((share, wide), F32),
+    )
+    kept = outputs[:4] + (((2, share, wide), F32),)
     results = pl.pallas_call(
         functools.partial(kernel, (n_resp, n_tensor, z_size, heads)),
-        out_shape=(
-            shape((seq, width), BF16),
-            shape((seq, width), BF16),
-            shape((seq, HD), BF16),
-            shape((seq, HD), BF16),
-            shape((share, wide), F32),
-            shape((share, wide), F32),
-        ),
+        out_shape=tuple(pltpu.VMEM(size, kind) for size, kind in kept),
         in_specs=[pl.BlockSpec(memory_space=pltpu.SMEM)] + [hbm] * 6,
-        out_specs=(hbm, hbm, vmem, vmem, vmem, vmem),
+        out_specs=(vmem,) * len(kept),
         scratch_shapes=[
             pltpu.VMEM((seq, width), BF16),
             pltpu.VMEM((seq, width), BF16),
@@ -510,9 +573,7 @@
             pltpu.VMEM((heads, 8, seq), F32),
             pltpu.VMEM((heads, HD + ONES, seq), F32),
             pltpu.VMEM((heads, HD, seq), F32),
-            pltpu.VMEM((seq, width), BF16),
-            pltpu.VMEM((seq, width), BF16),
-            pltpu.VMEM((2, max(PAIR * CHUNK, seq), seq), F32),
+            pltpu.VMEM((2, max(PAIR * CHUNK, CHUNK + seq), seq), F32),
             pltpu.VMEM((2, CHUNK, seq), BF16),
             pltpu.VMEM((2, CHUNK, seq), BF16),
             pltpu.VMEM((2, 8, seq), F32),
@@ -521,19 +582,21 @@
             pltpu.VMEM((n_resp, 2, CHUNK, HD), BF16),
             pltpu.VMEM((n_resp, 2, CHUNK, HD), BF16),
             pltpu.VMEM((2, CHUNK, HD), F32),
+            pltpu.VMEM((2, share, wide), BF16),
+            pltpu.VMEM((2, CHUNK, HD), BF16),
+            pltpu.VMEM((2, share, wide), BF16),
             dma((6,)),
-            dma((2,)),
-            dma((n_tensor, 2)),
-            dma((n_tensor, 2)),
+            dma((3, n_tensor)),
+            dma((3, n_tensor)),
             dma((n_resp,)),
             dma((n_resp,)),
             dma((n_resp,)),
             dma((n_resp,)),
-            dma((n_tensor, 2)),
-            dma((n_tensor, 2)),
+            dma((n_tensor,)),
+            dma((n_tensor,)),
         ],
         compiler_params=pltpu.CompilerParams(
-            collective_id=0, has_side_effects=True, vmem_limit_bytes=60 * 2**20
+            collective_id=0, has_side_effects=True, vmem_limit_bytes=VMEM_BYTES
         ),
     )(
         lengths,
@@ -544,6 +607,14 @@
         prompt_keys,
         prompt_values,
     )
+    results = pl.pallas_call(
+        deliver,
+        out_shape=tuple(shape(size, kind) for size, kind in outputs),
+        in_specs=[vmem] * len(kept),
+        out_specs=(hbm,) * len(outputs),
+        scratch_shapes=[dma((len(outputs),))],
+        compiler_params=pltpu.CompilerParams(vmem_limit_bytes=2**20),
+    )(*results)
     attended, query_grad, key_grad, value_grad, prompt_key_grad, prompt_value_grad = results
     return (
         attended[None],

time: 72.1 us -> 58.4 us (0.81)
  local copies, waits for them, and re-layouts: 6.88 us -> 0 us
  Pallas kernels: 63.5 us -> 56.8 us
    pallas_call x1, Pallas kernels: 63.5 us -> 55.3 us  [per_device(): pl.pallas_call(functools.partial(kernel, (n_resp, n_tensor, z_size, heads...]
    unnamed x16 -> x0, local copies, waits for them, and re-layouts: 6.88 us -> none
    pallas_call x0 -> x1, Pallas kernels: none -> 1.53 us  [per_device(): pl.pallas_call(deliver, out_shape=tuple((shape(size, kind) for size, kind...]
where the time goes in v2:
time: 58.4 us; the launch traced here: 58.3 us
  Pallas kernels  56.8 us (97%)
  between operations  1.45 us (2%)
    pallas_call x1, Pallas kernels, per_device(): pl.pallas_call(functools.partial(kernel, (n_resp, n_tensor, z_size, heads...  55.3 us
    pallas_call x1, Pallas kernels, per_device(): pl.pallas_call(deliver, out_shape=tuple((shape(size, kind) for size, kind...  1.53 us

profile of v2, /device:TPU:1, one launch (start us, length us, event | category | flops | bytes accessed | tf_op | source)
XLA Modules:
  0.0 58.3 jit_solution(2311076122478262186)
XLA Ops:
  1.3 55.3 %shard_map.118 = (bf16[512,1024]{1,0:T(8,128)(2,1)S(1)}, bf16[512,1024]{1,0:T(8,128)(2,1)S(1)}, bf16[512,128]{1,0:T(8,128)(2,1)S(1)}, bf16[512,128]{1,0:T(8,128)(2,1)S(1)}, f32[2,32,1024]{2,1,0:T(8,128)S(1)}) custom-call(s32[1]{0:T(128)S(6)} %copy.13.length_ref, bf16[512,1024]{1,0:T(8,128)(2,1)} %bitcast.8, bf16[512,1024]{1,0:T(8,128)(2,1)} %bitcast.9, ...), custom_call_target="tpu_custom_call" | custom-call | tf_op jit(solution)/shard_map/pallas_call | solution.py:553
  56.6 1.5 %shard_map.119 = (bf16[512,1024]{1,0:T(8,128)(2,1)}, bf16[512,1024]{1,0:T(8,128)(2,1)}, bf16[512,128]{1,0:T(8,128)(2,1)}, bf16[512,128]{1,0:T(8,128)(2,1)}, f32[32,1024]{1,0:T(8,128)}, /*index=5*/f32[32,1024]{1,0:T(8,128)}) custom-call(bf16[512,1024]{1,0:T(8,128)(2,1)S(1)} %get-tuple-element.17.att, bf16[512,1024]{1,0:T(8,128)(2,1)S(1)} %get-tuple-element.18.dq, ...), custom_call_target="tpu_custom_call" | custom-call | tf_op jit(solution)/shard_map/pallas_call | solution.py:610
